TPU v7x, 32 devices: a whole 2x2x4 slice. The times are simulated.
32 devices in a mesh: groups: 2 (over y), ctx: 4 (over z), tp: 2 (over x), sub: 2 (over core).
Axes of the slice: x: 2, y: 2, z: 4, core: 2. Of those that a mesh axis runs over, the one named last changes fastest.
Arguments:
- queries: bfloat16 [4096, 8192], P(('groups', 'ctx'), ('tp', 'sub')), parts along dimension 0, may hold values from -6 to 6
- prompt_kv: bfloat16 [4096, 2048], P(('groups', 'ctx'), ('tp', 'sub')), parts along dimension 0, may hold values from -6 to 6
- resp_kv: bfloat16 [4096, 2048], P(('groups', 'ctx'), ('tp', 'sub')), parts along dimension 0, may hold values from -6 to 6
- block_resp: int32 [16], P('groups'), parts along dimension 0, may hold values from 0 to 3, as said below
- block_pos: int32 [16], P('groups'), parts along dimension 0, may hold values from 0 to 3
Outputs:
- attended: bfloat16 [4096, 8192], P(('groups', 'ctx'), ('tp', 'sub')), parts along dimension 0
There are 2 independent parts, one for each index of `groups`. A program takes and returns all parts, laid end to end along the dimension named above; each array names one. Nothing has to cross between parts.
Inputs may be any that keep to these rules, and one draw needn't show every extreme that they name: block_resp and block_pos place every block of every response in exactly one slot: response r has a length of 1 to 4 blocks, some response exactly 4, and one slot for each of its positions 0 to its length - 1; response r belongs to prompt r // 4.
All inputs are finite; a program needn't handle non-finite values.
Results may differ from a plain program's by a relative error of at most 0.0065.
Values may be sent and summed in bfloat16 or wider, within the bound.
A program may use at most 128 MiB of HBM per device.

v0:
```python
import math

import jax
import jax.numpy as jnp
from jax import lax
from jax.sharding import PartitionSpec as P

HD = 128
QH = 64
KVH = 8
BLK = 256
PLEN = 2048
GEN = 4
MAXB = 4


def shards(queries, prompt_kv, resp_kv, block_resp, block_pos):
    rows = queries.shape[0]
    nloc = rows // BLK
    width = prompt_kv.shape[1]
    kvloc = width // (2 * HD)
    group = QH // KVH
    qloc = kvloc * group
    nblk = block_resp.shape[0]
    scale = 1.0 / math.sqrt(HD)
    slots_here = lax.axis_index("ctx") * nloc + jnp.arange(nloc, dtype=jnp.int32)
    resp_here = block_resp[slots_here]
    pos_here = block_pos[slots_here]
    qheads = queries.reshape(nloc, BLK, qloc, HD).transpose(2, 0, 1, 3)
    within = jnp.arange(BLK, dtype=jnp.int32)
    all_prompt, all_answer = (
        lax.all_gather(prompt_kv, "ctx", axis=0, tiled=True),
        lax.all_gather(resp_kv, "ctx", axis=0, tiled=True),
    )
    answer_blocks = all_answer.reshape(nblk, BLK, width)
    positions = jnp.arange(MAXB, dtype=jnp.int32)
    hit = (block_resp[None, None, :] == resp_here[:, None, None]) & (
        block_pos[None, None, :] == positions[None, :, None]
    )
    table = jnp.sum(jnp.where(hit, jnp.arange(nblk, dtype=jnp.int32)[None, None, :], 0), axis=-1)
    prompt_rows = jnp.stack(
        [
            lax.dynamic_slice_in_dim(all_prompt, resp_here[slot] // GEN * PLEN, PLEN, 0)
            for slot in range(nloc)
        ]
    )
    answer_rows = answer_blocks[table].reshape(nloc, MAXB * BLK, width)
    keyvals = jnp.concatenate([prompt_rows, answer_rows], axis=1).reshape(
        nloc, PLEN + MAXB * BLK, kvloc, 2, HD
    )
    keys = keyvals[:, :, :, 0].transpose(2, 0, 1, 3)
    values = keyvals[:, :, :, 1].transpose(2, 0, 1, 3)
    which = jnp.repeat(positions, BLK)
    inner = jnp.tile(within, MAXB)
    answer_mask = (which[None, None, :] < pos_here[:, None, None]) | (
        which[None, None, :] == pos_here[:, None, None]
    ) & (inner[None, None, :] <= within[None, :, None])
    mask = jnp.concatenate([jnp.ones((nloc, BLK, PLEN), dtype=bool), answer_mask], axis=2)

    def one_head(index):
        owner = index // group
        scores = (
            jnp.einsum(
                "btd,bld->btl", qheads[index], keys[owner], preferred_element_type=jnp.float32
            )
            * scale
        )
        scores = jnp.where(mask, scores, -1e30)
        peak = jnp.max(scores, axis=-1, keepdims=True)
        expo = jnp.exp(scores - peak)
        total = jnp.sum(expo, axis=-1, keepdims=True)
        probs = expo.astype(jnp.bfloat16)
        mixed = (
            jnp.einsum("btl,bld->btd", probs, values[owner], preferred_element_type=jnp.float32)
            / total
        )
        return mixed.astype(jnp.bfloat16)

    outputs = lax.map(one_head, jnp.arange(qloc, dtype=jnp.int32))
    return outputs.transpose(1, 2, 0, 3).reshape(rows, qloc * HD)


def solution(mesh):
    in_specs = (
        P(("groups", "ctx"), ("tp", "sub")),
        P(("groups", "ctx"), ("tp", "sub")),
        P(("groups", "ctx"), ("tp", "sub")),
        P("groups"),
        P("groups"),
    )
    out_specs = P(("groups", "ctx"), ("tp", "sub"))
    return jax.shard_map(shards, mesh=mesh, in_specs=in_specs, out_specs=out_specs, check_vma=False)
```

profile of v0, /device:TPU:0, one launch (start us, length us, event | category | flops | bytes accessed | tf_op | source)
XLA Modules:
  0.0 309.1 jit_solution(3460227906629607399)
XLA Ops:
  17.1 40.5 %all-gather.5.cloned.1.call-done = bf16[2048,512]{1,0:T(8,128)(2,1)} async-done(((bf16[512,512]{1,0:T(8,128)(2,1)}), bf16[2048,512]{1,0:T(8,128)(2,1)}) %all-gather.5.cloned.1.call-update) | async-done | bytes 2097168 | tf_op jit(solution)/shard_map/all_gather | solution.py:33
  57.6 3.6 %gather_fusion.1 = bf16[8,256,512]{2,1,0:T(8,128)(2,1)} fusion(bf16[8,256,512]{2,1,0:T(8,128)(2,1)} %bitcast.76, s32[1024]{0:T(1024)S(1)} %pad_clamp_fusion), kind=kCustom, calls=%fused_computation.1 | custom fusion | bytes 4194336 | tf_op jit(solution)/shard_map/gather | solution.py:47
  61.2 4.0 %concatenate.10 = bf16[2,1024,2,2,128]{4,3,2,1,0:T(2,128)(2,1)} reshape(bf16[8,256,512]{2,1,0:T(8,128)(2,1)} %gather_fusion.1) | data formatting | bytes 4194304 | tf_op jit(solution)/shard_map/concatenate | solution.py:48
  65.2 6.2 %copy.14 = bf16[2,1024,2,2,128]{1,4,3,2,0:T(8,128)(2,1)} copy(bf16[2,1024,2,2,128]{4,3,2,1,0:T(2,128)(2,1)} %concatenate.10) | data formatting | bytes 4194304 | tf_op jit(solution)/shard_map/concatenate | solution.py:48
  71.4 32.4 %all-gather.3.cloned.1.call-done = bf16[2048,512]{0,1:T(8,128)(2,1)} async-done(((bf16[512,512]{0,1:T(8,128)(2,1)}), bf16[2048,512]{0,1:T(8,128)(2,1)}) %all-gather.3.cloned.1.call-update) | async-done | bytes 2097168 | tf_op jit(solution)/shard_map/all_gather | solution.py:32
  103.9 5.4 %pad_maximum_fusion = bf16[2,3072,2,2,128]{1,4,3,2,0:T(8,128)(2,1)S(1)} fusion(bf16[2,1024,2,2,128]{1,4,3,2,0:T(8,128)(2,1)} %copy.14, bf16[1,2048,2,2,128]{1,4,3,2,0:T(8,128)(2,1)} %bitcast.75), kind=kLoop, calls=%fused_computation.21 | loop fusion | flops 18874368 | bytes 10485760 | tf_op jit(solution)/shard_map/concatenate | solution.py:48
  109.3 3.4 %slice_bitcast_fusion = (bf16[2,2,3072,128]{2,3,0,1:T(8,128)(2,1)}, bf16[2,2,3072,128]{2,3,0,1:T(8,128)(2,1)}) fusion(bf16[2,3072,2,2,128]{1,4,3,2,0:T(8,128)(2,1)S(1)} %pad_maximum_fusion), kind=kLoop, calls=%fused_computation.22 | loop fusion | bytes 12582912 | tf_op jit(solution)/shard_map/transpose | solution.py:52
  112.7 184.7 %while.12 = (s32[]{:T(128)}, bf16[16,2,256,128]{3,2,1,0:T(8,128)(2,1)}, s32[16]{0:T(128)S(1)}, bf16[16,2,256,128]{3,2,1,0:T(8,128)(2,1)}, bf16[2,2,3072,128]{2,3...) while((s32[]{:T(128)}, ...), condition=%wide.region_4.5_spmd, body=%wide.region_1.4_spmd.sunk | while | flops 816446464 | bytes 36449160 | solution.py:79
  117.4 3.2 %fusion.42 = (f32[2,256]{1,0:T(2,128)S(1)}, f32[2,256,3072]{2,1,0:T(8,128)S(1)}) fusion(pred[2,256,3072]{2,1,0:T(32,128)(4,1)S(1)} %get-tuple-element.210, bf16[2,2,3072,128]{2,3,0,1:T(8,128)(2,1)} %get-tuple-element.209, s32[]{:T(128)S(6)} %select_n.70, bf16[16,2,256,128]{3,2,1,0:T(8,128)(2,1)} %get-tuple-element.208, s32[]{:T(128)S(6)} %select_n.71), kind=kOutput, calls=%fused_computation.40.clone.1 | convolution fusion | flops 407371264 | bytes 9570312 | tf_op jit(solution)/shard_map/while/body/eval_jaxpr/btd,bld->btl/dot_general | solution.py:63
  129.0 3.2 %fusion.42 = (f32[2,256]{1,0:T(2,128)S(1)}, f32[2,256,3072]{2,1,0:T(8,128)S(1)}) fusion(pred[2,256,3072]{2,1,0:T(32,128)(4,1)S(1)} %get-tuple-element.210, bf16[2,2,3072,128]{2,3,0,1:T(8,128)(2,1)} %get-tuple-element.209, s32[]{:T(128)S(6)} %select_n.70, bf16[16,2,256,128]{3,2,1,0:T(8,128)(2,1)} %get-tuple-element.208, s32[]{:T(128)S(6)} %select_n.71), kind=kOutput, calls=%fused_computation.40.clone.1 | convolution fusion | flops 407371264 | bytes 9570312 | tf_op jit(solution)/shard_map/while/body/eval_jaxpr/btd,bld->btl/dot_general | solution.py:63
  140.5 3.1 %fusion.42 = (f32[2,256]{1,0:T(2,128)S(1)}, f32[2,256,3072]{2,1,0:T(8,128)S(1)}) fusion(pred[2,256,3072]{2,1,0:T(32,128)(4,1)S(1)} %get-tuple-element.210, bf16[2,2,3072,128]{2,3,0,1:T(8,128)(2,1)} %get-tuple-element.209, s32[]{:T(128)S(6)} %select_n.70, bf16[16,2,256,128]{3,2,1,0:T(8,128)(2,1)} %get-tuple-element.208, s32[]{:T(128)S(6)} %select_n.71), kind=kOutput, calls=%fused_computation.40.clone.1 | convolution fusion | flops 407371264 | bytes 9570312 | tf_op jit(solution)/shard_map/while/body/eval_jaxpr/btd,bld->btl/dot_general | solution.py:63
  152.1 3.2 %fusion.42 = (f32[2,256]{1,0:T(2,128)S(1)}, f32[2,256,3072]{2,1,0:T(8,128)S(1)}) fusion(pred[2,256,3072]{2,1,0:T(32,128)(4,1)S(1)} %get-tuple-element.210, bf16[2,2,3072,128]{2,3,0,1:T(8,128)(2,1)} %get-tuple-element.209, s32[]{:T(128)S(6)} %select_n.70, bf16[16,2,256,128]{3,2,1,0:T(8,128)(2,1)} %get-tuple-element.208, s32[]{:T(128)S(6)} %select_n.71), kind=kOutput, calls=%fused_computation.40.clone.1 | convolution fusion | flops 407371264 | bytes 9570312 | tf_op jit(solution)/shard_map/while/body/eval_jaxpr/btd,bld->btl/dot_general | solution.py:63
  163.6 3.1 %fusion.42 = (f32[2,256]{1,0:T(2,128)S(1)}, f32[2,256,3072]{2,1,0:T(8,128)S(1)}) fusion(pred[2,256,3072]{2,1,0:T(32,128)(4,1)S(1)} %get-tuple-element.210, bf16[2,2,3072,128]{2,3,0,1:T(8,128)(2,1)} %get-tuple-element.209, s32[]{:T(128)S(6)} %select_n.70, bf16[16,2,256,128]{3,2,1,0:T(8,128)(2,1)} %get-tuple-element.208, s32[]{:T(128)S(6)} %select_n.71), kind=kOutput, calls=%fused_computation.40.clone.1 | convolution fusion | flops 407371264 | bytes 9570312 | tf_op jit(solution)/shard_map/while/body/eval_jaxpr/btd,bld->btl/dot_general | solution.py:63
  175.2 3.2 %fusion.42 = (f32[2,256]{1,0:T(2,128)S(1)}, f32[2,256,3072]{2,1,0:T(8,128)S(1)}) fusion(pred[2,256,3072]{2,1,0:T(32,128)(4,1)S(1)} %get-tuple-element.210, bf16[2,2,3072,128]{2,3,0,1:T(8,128)(2,1)} %get-tuple-element.209, s32[]{:T(128)S(6)} %select_n.70, bf16[16,2,256,128]{3,2,1,0:T(8,128)(2,1)} %get-tuple-element.208, s32[]{:T(128)S(6)} %select_n.71), kind=kOutput, calls=%fused_computation.40.clone.1 | convolution fusion | flops 407371264 | bytes 9570312 | tf_op jit(solution)/shard_map/while/body/eval_jaxpr/btd,bld->btl/dot_general | solution.py:63
  186.7 3.1 %fusion.42 = (f32[2,256]{1,0:T(2,128)S(1)}, f32[2,256,3072]{2,1,0:T(8,128)S(1)}) fusion(pred[2,256,3072]{2,1,0:T(32,128)(4,1)S(1)} %get-tuple-element.210, bf16[2,2,3072,128]{2,3,0,1:T(8,128)(2,1)} %get-tuple-element.209, s32[]{:T(128)S(6)} %select_n.70, bf16[16,2,256,128]{3,2,1,0:T(8,128)(2,1)} %get-tuple-element.208, s32[]{:T(128)S(6)} %select_n.71), kind=kOutput, calls=%fused_computation.40.clone.1 | convolution fusion | flops 407371264 | bytes 9570312 | tf_op jit(solution)/shard_map/while/body/eval_jaxpr/btd,bld->btl/dot_general | solution.py:63
  198.3 3.2 %fusion.42 = (f32[2,256]{1,0:T(2,128)S(1)}, f32[2,256,3072]{2,1,0:T(8,128)S(1)}) fusion(pred[2,256,3072]{2,1,0:T(32,128)(4,1)S(1)} %get-tuple-element.210, bf16[2,2,3072,128]{2,3,0,1:T(8,128)(2,1)} %get-tuple-element.209, s32[]{:T(128)S(6)} %select_n.70, bf16[16,2,256,128]{3,2,1,0:T(8,128)(2,1)} %get-tuple-element.208, s32[]{:T(128)S(6)} %select_n.71), kind=kOutput, calls=%fused_computation.40.clone.1 | convolution fusion | flops 407371264 | bytes 9570312 | tf_op jit(solution)/shard_map/while/body/eval_jaxpr/btd,bld->btl/dot_general | solution.py:63
  209.8 3.1 %fusion.42 = (f32[2,256]{1,0:T(2,128)S(1)}, f32[2,256,3072]{2,1,0:T(8,128)S(1)}) fusion(pred[2,256,3072]{2,1,0:T(32,128)(4,1)S(1)} %get-tuple-element.210, bf16[2,2,3072,128]{2,3,0,1:T(8,128)(2,1)} %get-tuple-element.209, s32[]{:T(128)S(6)} %select_n.70, bf16[16,2,256,128]{3,2,1,0:T(8,128)(2,1)} %get-tuple-element.208, s32[]{:T(128)S(6)} %select_n.71), kind=kOutput, calls=%fused_computation.40.clone.1 | convolution fusion | flops 407371264 | bytes 9570312 | tf_op jit(solution)/shard_map/while/body/eval_jaxpr/btd,bld->btl/dot_general | solution.py:63
  221.4 3.2 %fusion.42 = (f32[2,256]{1,0:T(2,128)S(1)}, f32[2,256,3072]{2,1,0:T(8,128)S(1)}) fusion(pred[2,256,3072]{2,1,0:T(32,128)(4,1)S(1)} %get-tuple-element.210, bf16[2,2,3072,128]{2,3,0,1:T(8,128)(2,1)} %get-tuple-element.209, s32[]{:T(128)S(6)} %select_n.70, bf16[16,2,256,128]{3,2,1,0:T(8,128)(2,1)} %get-tuple-element.208, s32[]{:T(128)S(6)} %select_n.71), kind=kOutput, calls=%fused_computation.40.clone.1 | convolution fusion | flops 407371264 | bytes 9570312 | tf_op jit(solution)/shard_map/while/body/eval_jaxpr/btd,bld->btl/dot_general | solution.py:63
  232.9 3.1 %fusion.42 = (f32[2,256]{1,0:T(2,128)S(1)}, f32[2,256,3072]{2,1,0:T(8,128)S(1)}) fusion(pred[2,256,3072]{2,1,0:T(32,128)(4,1)S(1)} %get-tuple-element.210, bf16[2,2,3072,128]{2,3,0,1:T(8,128)(2,1)} %get-tuple-element.209, s32[]{:T(128)S(6)} %select_n.70, bf16[16,2,256,128]{3,2,1,0:T(8,128)(2,1)} %get-tuple-element.208, s32[]{:T(128)S(6)} %select_n.71), kind=kOutput, calls=%fused_computation.40.clone.1 | convolution fusion | flops 407371264 | bytes 9570312 | tf_op jit(solution)/shard_map/while/body/eval_jaxpr/btd,bld->btl/dot_general | solution.py:63
  244.4 3.2 %fusion.42 = (f32[2,256]{1,0:T(2,128)S(1)}, f32[2,256,3072]{2,1,0:T(8,128)S(1)}) fusion(pred[2,256,3072]{2,1,0:T(32,128)(4,1)S(1)} %get-tuple-element.210, bf16[2,2,3072,128]{2,3,0,1:T(8,128)(2,1)} %get-tuple-element.209, s32[]{:T(128)S(6)} %select_n.70, bf16[16,2,256,128]{3,2,1,0:T(8,128)(2,1)} %get-tuple-element.208, s32[]{:T(128)S(6)} %select_n.71), kind=kOutput, calls=%fused_computation.40.clone.1 | convolution fusion | flops 407371264 | bytes 9570312 | tf_op jit(solution)/shard_map/while/body/eval_jaxpr/btd,bld->btl/dot_general | solution.py:63
  256.0 3.1 %fusion.42 = (f32[2,256]{1,0:T(2,128)S(1)}, f32[2,256,3072]{2,1,0:T(8,128)S(1)}) fusion(pred[2,256,3072]{2,1,0:T(32,128)(4,1)S(1)} %get-tuple-element.210, bf16[2,2,3072,128]{2,3,0,1:T(8,128)(2,1)} %get-tuple-element.209, s32[]{:T(128)S(6)} %select_n.70, bf16[16,2,256,128]{3,2,1,0:T(8,128)(2,1)} %get-tuple-element.208, s32[]{:T(128)S(6)} %select_n.71), kind=kOutput, calls=%fused_computation.40.clone.1 | convolution fusion | flops 407371264 | bytes 9570312 | tf_op jit(solution)/shard_map/while/body/eval_jaxpr/btd,bld->btl/dot_general | solution.py:63
  267.5 3.2 %fusion.42 = (f32[2,256]{1,0:T(2,128)S(1)}, f32[2,256,3072]{2,1,0:T(8,128)S(1)}) fusion(pred[2,256,3072]{2,1,0:T(32,128)(4,1)S(1)} %get-tuple-element.210, bf16[2,2,3072,128]{2,3,0,1:T(8,128)(2,1)} %get-tuple-element.209, s32[]{:T(128)S(6)} %select_n.70, bf16[16,2,256,128]{3,2,1,0:T(8,128)(2,1)} %get-tuple-element.208, s32[]{:T(128)S(6)} %select_n.71), kind=kOutput, calls=%fused_computation.40.clone.1 | convolution fusion | flops 407371264 | bytes 9570312 | tf_op jit(solution)/shard_map/while/body/eval_jaxpr/btd,bld->btl/dot_general | solution.py:63
  279.1 3.1 %fusion.42 = (f32[2,256]{1,0:T(2,128)S(1)}, f32[2,256,3072]{2,1,0:T(8,128)S(1)}) fusion(pred[2,256,3072]{2,1,0:T(32,128)(4,1)S(1)} %get-tuple-element.210, bf16[2,2,3072,128]{2,3,0,1:T(8,128)(2,1)} %get-tuple-element.209, s32[]{:T(128)S(6)} %select_n.70, bf16[16,2,256,128]{3,2,1,0:T(8,128)(2,1)} %get-tuple-element.208, s32[]{:T(128)S(6)} %select_n.71), kind=kOutput, calls=%fused_computation.40.clone.1 | convolution fusion | flops 407371264 | bytes 9570312 | tf_op jit(solution)/shard_map/while/body/eval_jaxpr/btd,bld->btl/dot_general | solution.py:63
  290.6 3.2 %fusion.42 = (f32[2,256]{1,0:T(2,128)S(1)}, f32[2,256,3072]{2,1,0:T(8,128)S(1)}) fusion(pred[2,256,3072]{2,1,0:T(32,128)(4,1)S(1)} %get-tuple-element.210, bf16[2,2,3072,128]{2,3,0,1:T(8,128)(2,1)} %get-tuple-element.209, s32[]{:T(128)S(6)} %select_n.70, bf16[16,2,256,128]{3,2,1,0:T(8,128)(2,1)} %get-tuple-element.208, s32[]{:T(128)S(6)} %select_n.71), kind=kOutput, calls=%fused_computation.40.clone.1 | convolution fusion | flops 407371264 | bytes 9570312 | tf_op jit(solution)/shard_map/while/body/eval_jaxpr/btd,bld->btl/dot_general | solution.py:63
  (115 shorter events, 84.1 us)
Async XLA Ops:
  6.5 2.9 copy-start
  6.5 51.1 %all-gather.5.cloned.1.call-start = ((), (), s32[]{:S(2)}) async-start(), calls=%async_computation.1 | async-start | bytes 2621440 | tf_op jit(solution)/shard_map/all_gather | solution.py:33
  7.3 96.6 %all-gather.3.cloned.1.call-start = ((), (), s32[]{:S(2)}) async-start(), calls=%async_computation | async-start | bytes 2621440 | tf_op jit(solution)/shard_map/all_gather | solution.py:32
  11.0 0.7 copy-start.1
  120.6 1.9 copy-start.2
  132.1 1.9 copy-start.2
  143.7 1.9 copy-start.2
  155.2 1.9 copy-start.2
  166.8 1.9 copy-start.2
  178.3 1.9 copy-start.2
  189.9 1.9 copy-start.2
  201.4 1.9 copy-start.2
  213.0 1.9 copy-start.2
  224.5 1.9 copy-start.2
  236.0 1.9 copy-start.2
  247.6 1.9 copy-start.2
  259.1 1.9 copy-start.2
  270.7 1.9 copy-start.2
  282.2 1.9 copy-start.2
  293.8 1.9 copy-start.2
Sparse Core Ops, SparseCore 0:
  8.9 48.6 all-gather.4
  59.2 44.6 all-gather.2
where the time goes:
time: 312 us; the launch traced here: 309 us
  matrix products  78.7 us (25%)
  waiting for transfers between devices  73.6 us (24%)
  loops' own time  65.4 us (21%)
  local copies, waits for them, and re-layouts  55.6 us (18%)
  other arithmetic  22.1 us (7%)
  between operations  13.5 us (4%)
    another operation x1, loops' own time, shards(): outputs = lax.map(one_head, jnp.arange(qloc, dtype=jnp.int32))  65.4 us
    dot_general x16, matrix products, one_head(): jnp.einsum('btd,bld->btl', qheads[index], keys[owner], preferred_element_...  50.4 us
    all_gather x1, waiting for transfers between devices, shards(): lax.all_gather(resp_kv, 'ctx', axis=0, tiled=True)  40.5 us
    all_gather x1, waiting for transfers between devices, shards(): lax.all_gather(prompt_kv, 'ctx', axis=0, tiled=True)  32.4 us
    dot_general x16, matrix products, one_head(): jnp.einsum('btl,bld->btd', probs, values[owner], preferred_element_type=j...  28.3 us
    reduce_sum x16, other arithmetic, one_head(): total = jnp.sum(expo, axis=-1, keepdims=True)  15.8 us
    while x32, local copies, waits for them, and re-layouts  14.4 us
    dynamic_slice x16, local copies, waits for them, and re-layouts, shards(): outputs = lax.map(one_head, jnp.arange(qloc, dtype=jnp.int32))  10.4 us
  transfers between devices with their start and end apart: 2, of which 2 were waited for; matrix products, arithmetic and copies ran while one was open for 8% of the time, Pallas kernels for 0%

commit v1 on v0

--- a/solution.py
+++ b/solution.py
@@ -3,6 +3,8 @@
 import jax
 import jax.numpy as jnp
 from jax import lax
+from jax.experimental import pallas as pl
+from jax.experimental.pallas import tpu as pltpu
 from jax.sharding import PartitionSpec as P
 
 HD = 128
@@ -80,6 +82,361 @@
     return outputs.transpose(1, 2, 0, 3).reshape(rows, qloc * HD)
 
 
+NT = (((1,), (1,)), ((), ()))
+TN = (((0,), (0,)), ((), ()))
+C2 = math.log2(math.e) / math.sqrt(HD)
+MESH = pl.DeviceIdType.MESH
+
+
+def kernel(
+    q_ref, p_ref, r_ref, resp_ref, pos_ref, o_ref,
+    pb, rb, eb, fb, q2, acc, m, l,
+    recv_p, recv_r, recv_e, send_e, send_o,
+):
+    me = lax.axis_index("ctx")
+    is_end = (me == 0) | (me == 3)
+    is_mid = (me == 1) | (me == 2)
+    low = me < 2
+    near = jnp.where(low, 0, 3)
+    other = jnp.where(low, 2, 1)
+    far = 3 - near
+    inner = jnp.where(me == 0, 1, jnp.where(me == 3, 2, other))
+
+    def p_at(src, half):
+        return pb.at[src, pl.ds(half * BLK, BLK)]
+
+    def p_copy(src, half, sem, to):
+        return pltpu.make_async_remote_copy(
+            src_ref=p_at(src, half), dst_ref=p_at(src, half), send_sem=sem,
+            recv_sem=recv_p.at[src, half], device_id={"ctx": to}, device_id_type=MESH,
+        )
+
+    def r_copy(src, half, sem, to):
+        return pltpu.make_async_remote_copy(
+            src_ref=rb.at[src, half], dst_ref=rb.at[src, half], send_sem=sem,
+            recv_sem=recv_r.at[src, half], device_id={"ctx": to}, device_id_type=MESH,
+        )
+
+    def e_copy(k, sem, to):
+        return pltpu.make_async_remote_copy(
+            src_ref=eb.at[k], dst_ref=eb.at[k], send_sem=sem,
+            recv_sem=recv_e.at[k], device_id={"ctx": to}, device_id_type=MESH,
+        )
+
+    def got_p(src, half):
+        p_copy(src, half, send_o.at[0], inner).wait_recv()
+
+    def got_r(src, half):
+        r_copy(src, half, send_o.at[0], inner).wait_recv()
+
+    def got_e(k):
+        e_copy(k, send_o.at[0], inner).wait_recv()
+
+    def own_p(half, sem, to):
+        return p_copy(me, half, sem, to)
+
+    barrier = pltpu.get_barrier_semaphore()
+    pl.semaphore_signal(barrier, inc=1, device_id={"ctx": inner}, device_id_type=MESH)
+
+    @pl.when(is_mid)
+    def _():
+        pl.semaphore_signal(barrier, inc=1, device_id={"ctx": near}, device_id_type=MESH)
+
+    pb[me] = p_ref[...]
+    rb[me, 0] = r_ref[:BLK]
+    rb[me, 1] = r_ref[BLK:]
+
+    @pl.when(is_mid)
+    def _():
+        pl.semaphore_wait(barrier, 2)
+
+    @pl.when(is_end)
+    def _():
+        pl.semaphore_wait(barrier, 1)
+
+    @pl.when(is_mid)
+    def _():
+        for half in range(2):
+            own_p(half, send_e.at[half], near).start()
+
+    for half in range(2):
+        own_p(half, send_o.at[half], inner).start()
+    for half in range(2):
+        r_copy(me, half, send_o.at[2 + half], inner).start()
+
+    def needs(target, cand):
+        same = resp_ref[target] == resp_ref[cand]
+        return jnp.where(same & (pos_ref[cand] < pos_ref[target]), 1, 0)
+
+    def right_aligned(flags, count):
+        after = 0
+        ranks = []
+        for flag in reversed(flags):
+            ranks.append(count - 1 - after)
+            after = after + flag
+        ranks.reverse()
+        return [
+            [jnp.where(ranks[i] == k, flags[i], 0) for i in range(len(flags))]
+            for k in range(count)
+        ]
+
+    def choose(pick, blocks):
+        out = blocks[0]
+        for i in range(1, len(blocks)):
+            out = lax.select_n(pick[i] == 1, out, blocks[i])
+        return out
+
+    def end_picks(end, first, second, third):
+        cands = [2 * first, 2 * first + 1, 2 * second, 2 * second + 1, 2 * third, 2 * third + 1]
+        flags = [jnp.maximum(needs(2 * end, c), needs(2 * end + 1, c)) for c in cands]
+        return cands, right_aligned(flags, 4)
+
+    def send_entry(k, sem):
+        order = (me, other, far)
+        _, picks = end_picks(near, *order)
+        blocks = [rb[src, half] for src in order for half in range(2)][: k + 3]
+        eb[k] = choose(picks[k], blocks)
+        e_copy(k, sem, near).start()
+
+    def attend(k, v, base, bias=None, diag=False):
+        keys = k.shape[0]
+        k2 = jnp.concatenate([k, k], axis=1)
+        scores = [
+            lax.dot_general(k2, q2[base + u], NT, preferred_element_type=jnp.float32)
+            for u in range(QH // KVH)
+        ]
+        if diag:
+            key_at = lax.broadcasted_iota(jnp.int32, (keys, BLK), 0)
+            row_at = lax.broadcasted_iota(jnp.int32, (keys, BLK), 1)
+            seen = key_at <= row_at
+        for u, s in enumerate(scores):
+            i = base + u
+            if diag:
+                s = jnp.where(seen, s, -1e30)
+            peak = jnp.max(s, axis=0, keepdims=True)
+            if diag:
+                expo = jnp.exp2(s - peak)
+                l[i, 0:1] = jnp.sum(expo, axis=0, keepdims=True)
+                m[i, 0:1] = peak
+                acc[i] = lax.dot_general(
+                    v, expo.astype(jnp.bfloat16), TN, preferred_element_type=jnp.float32
+                )
+            else:
+                before = m[i, 0:1]
+                if bias is not None:
+                    peak = peak - bias
+                peak = jnp.maximum(before, peak)
+                expo = jnp.exp2(s - (peak if bias is None else peak + bias))
+                decay = jnp.exp2(before - peak)
+                l[i, 0:1] = l[i, 0:1] * decay + jnp.sum(expo, axis=0, keepdims=True)
+                m[i, 0:1] = peak
+                acc[i] = acc[i] * decay + lax.dot_general(
+                    v, expo.astype(jnp.bfloat16), TN, preferred_element_type=jnp.float32
+                )
+
+    def columns(head):
+        return (
+            pl.ds(pl.multiple_of(head * 2 * HD, 2 * HD), HD),
+            pl.ds(pl.multiple_of(head * 2 * HD + HD, HD), HD),
+        )
+
+    def q_at(i):
+        slot, head = i // 16, i % 16
+        return (
+            pl.ds(pl.multiple_of(slot * BLK, BLK), BLK),
+            pl.ds(pl.multiple_of(head * HD, HD), HD),
+        )
+
+    @pl.loop(0, 32)
+    def _(i):
+        rows, cols = q_at(i)
+        scaled = q_ref[rows, cols].astype(jnp.float32) * C2
+        high = scaled.astype(jnp.bfloat16)
+        rest = (scaled - high.astype(jnp.float32)).astype(jnp.bfloat16)
+        q2[i] = jnp.concatenate([high, rest], axis=1)
+
+    @pl.loop(0, 4)
+    def _(it):
+        slot, head = it // 2, it % 2
+        kc, vc = columns(head)
+        rows = pl.ds(pl.multiple_of(slot * BLK, BLK), BLK)
+        attend(r_ref[rows, kc], r_ref[rows, vc], slot * 16 + head * 8, diag=True)
+
+    def at(it, tick, role, action):
+        pl.when((it == tick) & role)(action)
+
+    def pass_p(src, half, sem, to):
+        def go():
+            got_p(src, half)
+            p_copy(src, half, sem, to).start()
+        return go
+
+    def pass_r(src, half, sem, to):
+        def go():
+            got_r(src, half)
+            r_copy(src, half, sem, to).start()
+        return go
+
+    def take_entry(half, k, sem, src):
+        def go():
+            got_r(src, half)
+            send_entry(k, sem)
+        return go
+
+    def take_p(src):
+        def go():
+            got_p(src, 0)
+            got_p(src, 1)
+        return go
+
+    def prompt_step(it):
+        step = it // 4
+        second = jnp.where(low, 1 - me, 5 - me)
+        third = jnp.where(low, 2, 1)
+        fourth = jnp.where(low, 3, 0)
+        src = jnp.where(
+            step == 0, me, jnp.where(step == 1, second, jnp.where(step == 2, third, fourth))
+        )
+        at(it, 1, is_mid, pass_p(other, 0, send_e.at[2], near))
+        at(it, 1, is_mid, pass_p(near, 0, send_o.at[4], other))
+        at(it, 4, is_mid, pass_p(other, 1, send_e.at[3], near))
+        at(it, 4, is_mid, pass_p(near, 1, send_o.at[5], other))
+        at(it, 6, is_mid, take_entry(0, 0, send_e.at[4], other))
+        at(it, 7, is_mid, pass_r(near, 0, send_o.at[6], other))
+        at(it, 9, is_mid, take_entry(1, 1, send_e.at[5], other))
+        at(it, 9, is_mid, pass_r(near, 1, send_o.at[7], other))
+        at(it, 11, is_mid, pass_p(far, 0, send_e.at[6], near))
+        at(it, 12, is_mid, pass_p(far, 1, send_e.at[7], near))
+        at(it, 4, is_end, take_p(second))
+        at(it, 8, is_end, take_p(third))
+        at(it, 12, is_end, take_p(fourth))
+        slot, head = (it % 4) // 2, it % 2
+        kc, vc = columns(head)
+        attend(pb[src, :, kc], pb[src, :, vc], slot * 16 + head * 8)
+
+    def fill(k):
+        used = []
+        for slot in range(2):
+            mine, sib = 2 * me + slot, 2 * me + 1 - slot
+
+            order = (near, other, far)
+            cands = [2 * src + half for src in order for half in range(2)]
+            flags = [needs(mine, sib)] + [needs(mine, c) for c in cands]
+            mid_pick = right_aligned(flags, 3)[k]
+
+            ends, picks = end_picks(me, inner, jnp.where(low, 2, 1), jnp.where(low, 3, 0))
+            flags = [needs(mine, sib)]
+            for entry in range(4):
+                flag = 0
+                for i, c in enumerate(ends):
+                    flag = flag + picks[entry][i] * needs(mine, c)
+                flags.append(flag)
+            end_pick = right_aligned(flags, 3)[k]
+
+            def fill_mid():
+                blocks = [rb[me, 1 - slot]]
+                blocks += [rb[src, half] for src in order for half in range(2)][: k + 4]
+                fb[slot] = choose(mid_pick, blocks)
+
+            def fill_end():
+                blocks = [rb[me, 1 - slot]] + [eb[entry] for entry in range(k + 2)]
+                fb[slot] = choose(end_pick, blocks)
+
+            pl.when(is_mid)(fill_mid)
+            pl.when(is_end)(fill_end)
+            used.append(jnp.where(is_mid, sum(mid_pick), sum(end_pick)))
+        biases = [jnp.where(u == 1, 0.0, 1e30).astype(jnp.float32) for u in used]
+
+        @pl.loop(0, 4)
+        def _(it):
+            slot, head = it // 2, it % 2
+            kc, vc = columns(head)
+            bias = jnp.where(slot == 0, biases[0], biases[1])
+            attend(fb[slot, :, kc], fb[slot, :, vc], slot * 16 + head * 8, bias=bias)
+
+    pl.loop(0, 12)(prompt_step)
+
+    @pl.when(is_end)
+    def _():
+        got_e(0)
+        got_e(1)
+
+    fill(0)
+    pl.loop(12, 16)(prompt_step)
+    pl.when(is_mid)(take_entry(0, 2, send_e.at[8], far))
+    pl.when(is_end)(lambda: got_e(2))
+    fill(1)
+    pl.when(is_mid)(take_entry(1, 3, send_e.at[9], far))
+    pl.when(is_end)(lambda: got_e(3))
+    fill(2)
+
+    @pl.loop(0, 32)
+    def _(i):
+        rows, cols = q_at(i)
+        o_ref[rows, cols] = (acc[i] / l[i, 0:1]).T.astype(o_ref.dtype)
+
+    for half in range(2):
+        own_p(half, send_o.at[half], inner).wait_send()
+        r_copy(me, half, send_o.at[2 + half], inner).wait_send()
+
+    @pl.when(is_mid)
+    def _():
+        for half in range(2):
+            own_p(half, send_e.at[half], near).wait_send()
+            p_copy(other, half, send_e.at[2 + half], near).wait_send()
+            e_copy(half, send_e.at[4 + half], near).wait_send()
+            p_copy(far, half, send_e.at[6 + half], near).wait_send()
+            e_copy(2 + half, send_e.at[8 + half], near).wait_send()
+            p_copy(near, half, send_o.at[4 + half], other).wait_send()
+            r_copy(near, half, send_o.at[6 + half], other).wait_send()
+
+
+def line_of_four(queries, prompt_kv, resp_kv, block_resp, block_pos):
+    rows, cols = queries.shape
+    width = prompt_kv.shape[1]
+    vmem = pl.BlockSpec(memory_space=pltpu.VMEM)
+    smem = pl.BlockSpec(memory_space=pltpu.SMEM)
+    heads = cols // HD
+    tiles = rows // BLK * heads
+    return pl.pallas_call(
+        kernel,
+        out_shape=jax.ShapeDtypeStruct((rows, cols), jnp.bfloat16),
+        in_specs=[vmem, vmem, vmem, smem, smem],
+        out_specs=vmem,
+        scratch_shapes=[
+            pltpu.VMEM((4, 2 * BLK, width), jnp.bfloat16),
+            pltpu.VMEM((4, 2, BLK, width), jnp.bfloat16),
+            pltpu.VMEM((4, BLK, width), jnp.bfloat16),
+            pltpu.VMEM((2, BLK, width), jnp.bfloat16),
+            pltpu.VMEM((tiles, BLK, 2 * HD), jnp.bfloat16),
+            pltpu.VMEM((tiles, HD, BLK), jnp.float32),
+            pltpu.VMEM((tiles, 8, BLK), jnp.float32),
+            pltpu.VMEM((tiles, 8, BLK), jnp.float32),
+            pltpu.SemaphoreType.DMA((4, 2)),
+            pltpu.SemaphoreType.DMA((4, 2)),
+            pltpu.SemaphoreType.DMA((4,)),
+            pltpu.SemaphoreType.DMA((10,)),
+            pltpu.SemaphoreType.DMA((8,)),
+        ],
+        compiler_params=pltpu.CompilerParams(
+            collective_id=0, has_side_effects=True, vmem_limit_bytes=56 * 2**20
+        ),
+        name="line_attention",
+    )(queries, prompt_kv, resp_kv, block_resp, block_pos)
+
+
+def shards_of(queries, prompt_kv, resp_kv, block_resp, block_pos):
+    ctx = lax.axis_size("ctx")
+    fits = (
+        ctx == 4
+        and queries.shape == (2 * BLK, 2 * (QH // KVH) * HD)
+        and prompt_kv.shape == (PLEN // 4, 4 * HD)
+        and resp_kv.shape == (2 * BLK, 4 * HD)
+    )
+    run = line_of_four if fits else shards
+    return run(queries, prompt_kv, resp_kv, block_resp, block_pos)
+
+
 def solution(mesh):
     in_specs = (
         P(("groups", "ctx"), ("tp", "sub")),
@@ -89,4 +446,4 @@
         P("groups"),
     )
     out_specs = P(("groups", "ctx"), ("tp", "sub"))
-    return jax.shard_map(shards, mesh=mesh, in_specs=in_specs, out_specs=out_specs, check_vma=False)
+    return jax.shard_map(shards_of, mesh=mesh, in_specs=in_specs, out_specs=out_specs, check_vma=False)

time: 312 us -> 76 us (0.24)
  matrix products: 78.7 us -> 0 us
  waiting for transfers between devices: 73.6 us -> 0 us
  Pallas kernels: 0 us -> 72.7 us
  loops' own time: 65.4 us -> 0 us
  local copies, waits for them, and re-layouts: 55.6 us -> 3.16 us
  other arithmetic: 22.1 us -> 0 us
  between operations: 13.5 us -> 0.01 us
    dot_general x32 -> x0, matrix products: 78.7 us -> none  [the longest x16 50.4 us: one_head(): jnp.einsum('btd,bld->btl', qheads[index], keys[owner], preferred_element_...]
    all_gather x2 -> x0, waiting for transfers between devices: 72.9 us -> none  [the longest x1 40.5 us: shards(): lax.all_gather(resp_kv, 'ctx', axis=0, tiled=True)]
    pallas_call x0 -> x1, Pallas kernels: none -> 72.7 us  [line_of_four(): pl.pallas_call(kernel, out_shape=jax.ShapeDtypeStruct((rows, cols), jnp.b...]
    another operation x1 -> x0, loops' own time: 65.4 us -> none  [shards(): outputs = lax.map(one_head, jnp.arange(qloc, dtype=jnp.int32))]
    while x33 -> x0, local copies, waits for them, and re-layouts: 16.3 us -> none
    reduce_sum x17 -> x0, other arithmetic: 16 us -> none  [the longest x16 15.8 us: one_head(): total = jnp.sum(expo, axis=-1, keepdims=True)]
    concatenate x3 -> x0, local copies, waits for them, and re-layouts: 10.5 us -> none  [the longest x2 10.2 us: shards(): jnp.concatenate([prompt_rows, answer_rows], axis=1)]
    dynamic_slice x16 -> x0, local copies, waits for them, and re-layouts: 10.4 us -> none  [shards(): outputs = lax.map(one_head, jnp.arange(qloc, dtype=jnp.int32))]
  transfers between devices with their start and end apart: 2 -> 0, of which waited for: 2 -> 0; matrix products, arithmetic and copies ran while one was open for 8% -> 0% of each run, Pallas kernels for 0% -> 0%
where the time goes in v1:
time: 76 us; the launch traced here: 75.9 us
  Pallas kernels  72.7 us (96%)
  local copies, waits for them, and re-layouts  3.16 us (4%)
    pallas_call x1, Pallas kernels, line_of_four(): pl.pallas_call(kernel, out_shape=jax.ShapeDtypeStruct((rows, cols), jnp.b...  72.7 us
    unnamed x1, local copies, waits for them, and re-layouts  3.16 us

profile of v1, /device:TPU:0, one launch (start us, length us, event | category | flops | bytes accessed | tf_op | source)
XLA Modules:
  0.0 75.9 jit_solution(17222967368978073314)
XLA Ops:
  0.0 72.7 %line_attention.1 = bf16[512,2048]{1,0:T(8,128)(2,1)} custom-call(bf16[512,2048]{1,0:T(8,128)(2,1)} %q_ref.1, bf16[512,512]{1,0:T(8,128)(2,1)} %p_ref.1, bf16[512,512]{1,0:T(8,128)(2,1)} %r_ref.1, s32[8]{0:T(128)} %resp_ref.1, s32[8]{0:T(128)} %pos_ref.1), custom_call_target="tpu_custom_call" | custom-call | tf_op jit(solution)/shard_map/line_attention/pallas_call | solution.py:401
  72.7 3.2 %copy.7 = bf16[512,2048]{1,0:T(8,128)(2,1)} copy(bf16[512,2048]{1,0:T(8,128)(2,1)} %line_attention.1) | data formatting | bytes 4194304

commit v2 on v1

--- a/solution.py
+++ b/solution.py
@@ -154,15 +154,14 @@
     def _():
         pl.semaphore_wait(barrier, 1)
 
-    @pl.when(is_mid)
-    def _():
-        for half in range(2):
+    def send_own(half):
+        own_p(half, send_o.at[half], inner).start()
+
+        @pl.when(is_mid)
+        def _():
             own_p(half, send_e.at[half], near).start()
 
-    for half in range(2):
-        own_p(half, send_o.at[half], inner).start()
-    for half in range(2):
-        r_copy(me, half, send_o.at[2 + half], inner).start()
+    send_own(0)
 
     def needs(target, cand):
         same = resp_ref[target] == resp_ref[cand]
@@ -255,8 +254,41 @@
         rest = (scaled - high.astype(jnp.float32)).astype(jnp.bfloat16)
         q2[i] = jnp.concatenate([high, rest], axis=1)
 
+    send_own(1)
+
+    def own_r(half):
+        own_p(half, send_o.at[half], inner).wait_send()
+        r_copy(me, half, send_o.at[2 + half], inner).start()
+
+    def event_early(half):
+        own_r(half)
+
+        @pl.when(is_mid)
+        def _():
+            got_p(other, half)
+            p_copy(other, half, send_e.at[2 + half], near).start()
+
+    def event_entry(half):
+        r_copy(me, half, send_o.at[2 + half], inner).wait_send()
+        got_p(near, half)
+        p_copy(near, half, send_o.at[4 + half], other).start()
+        got_r(other, half)
+        send_entry(half, send_e.at[4 + half])
+
+    def event_far_p(half):
+        p_copy(near, half, send_o.at[4 + half], other).wait_send()
+        got_r(near, half)
+        r_copy(near, half, send_o.at[6 + half], other).start()
+        got_p(far, half)
+        p_copy(far, half, send_e.at[6 + half], near).start()
+
+    def event_far_r(half):
+        got_r(far, half)
+        send_entry(2 + half, send_e.at[8 + half])
+
     @pl.loop(0, 4)
     def _(it):
+        pl.when(it == 2)(lambda: event_early(0))
         slot, head = it // 2, it % 2
         kc, vc = columns(head)
         rows = pl.ds(pl.multiple_of(slot * BLK, BLK), BLK)
@@ -264,24 +296,6 @@
 
     def at(it, tick, role, action):
         pl.when((it == tick) & role)(action)
-
-    def pass_p(src, half, sem, to):
-        def go():
-            got_p(src, half)
-            p_copy(src, half, sem, to).start()
-        return go
-
-    def pass_r(src, half, sem, to):
-        def go():
-            got_r(src, half)
-            r_copy(src, half, sem, to).start()
-        return go
-
-    def take_entry(half, k, sem, src):
-        def go():
-            got_r(src, half)
-            send_entry(k, sem)
-        return go
 
     def take_p(src):
         def go():
@@ -291,22 +305,18 @@
 
     def prompt_step(it):
         step = it // 4
-        second = jnp.where(low, 1 - me, 5 - me)
-        third = jnp.where(low, 2, 1)
+        second = jnp.where(is_end, inner, other)
+        third = jnp.where(is_end, jnp.where(low, 2, 1), near)
         fourth = jnp.where(low, 3, 0)
         src = jnp.where(
             step == 0, me, jnp.where(step == 1, second, jnp.where(step == 2, third, fourth))
         )
-        at(it, 1, is_mid, pass_p(other, 0, send_e.at[2], near))
-        at(it, 1, is_mid, pass_p(near, 0, send_o.at[4], other))
-        at(it, 4, is_mid, pass_p(other, 1, send_e.at[3], near))
-        at(it, 4, is_mid, pass_p(near, 1, send_o.at[5], other))
-        at(it, 6, is_mid, take_entry(0, 0, send_e.at[4], other))
-        at(it, 7, is_mid, pass_r(near, 0, send_o.at[6], other))
-        at(it, 9, is_mid, take_entry(1, 1, send_e.at[5], other))
-        at(it, 9, is_mid, pass_r(near, 1, send_o.at[7], other))
-        at(it, 11, is_mid, pass_p(far, 0, send_e.at[6], near))
-        at(it, 12, is_mid, pass_p(far, 1, send_e.at[7], near))
+        pl.when(it == 1)(lambda: event_early(1))
+        at(it, 3, is_mid, lambda: event_entry(0))
+        at(it, 6, is_mid, lambda: event_entry(1))
+        at(it, 9, is_mid, lambda: event_far_p(0))
+        at(it, 13, is_mid, lambda: event_far_r(0))
+        at(it, 15, is_mid, lambda: event_far_r(1))
         at(it, 4, is_end, take_p(second))
         at(it, 8, is_end, take_p(third))
         at(it, 12, is_end, take_p(fourth))
@@ -361,23 +371,22 @@
         got_e(0)
         got_e(1)
 
+    pl.when(is_mid)(lambda: event_far_p(1))
     fill(0)
     pl.loop(12, 16)(prompt_step)
-    pl.when(is_mid)(take_entry(0, 2, send_e.at[8], far))
     pl.when(is_end)(lambda: got_e(2))
     fill(1)
-    pl.when(is_mid)(take_entry(1, 3, send_e.at[9], far))
     pl.when(is_end)(lambda: got_e(3))
     fill(2)
 
     @pl.loop(0, 32)
     def _(i):
-        rows, cols = q_at(i)
-        o_ref[rows, cols] = (acc[i] / l[i, 0:1]).T.astype(o_ref.dtype)
-
-    for half in range(2):
-        own_p(half, send_o.at[half], inner).wait_send()
-        r_copy(me, half, send_o.at[2 + half], inner).wait_send()
+        o_ref[i] = (acc[i] / l[i, 0:1]).astype(o_ref.dtype)
+
+    @pl.when(is_end)
+    def _():
+        for half in range(2):
+            r_copy(me, half, send_o.at[2 + half], inner).wait_send()
 
     @pl.when(is_mid)
     def _():
@@ -387,8 +396,12 @@
             e_copy(half, send_e.at[4 + half], near).wait_send()
             p_copy(far, half, send_e.at[6 + half], near).wait_send()
             e_copy(2 + half, send_e.at[8 + half], near).wait_send()
-            p_copy(near, half, send_o.at[4 + half], other).wait_send()
             r_copy(near, half, send_o.at[6 + half], other).wait_send()
+
+
+def turn(x_ref, o_ref):
+    for u in range(x_ref.shape[0]):
+        o_ref[:, u * HD : (u + 1) * HD] = x_ref[u].T
 
 
 def line_of_four(queries, prompt_kv, resp_kv, block_resp, block_pos):
@@ -398,9 +411,9 @@
     smem = pl.BlockSpec(memory_space=pltpu.SMEM)
     heads = cols // HD
     tiles = rows // BLK * heads
-    return pl.pallas_call(
+    turned = pl.pallas_call(
         kernel,
-        out_shape=jax.ShapeDtypeStruct((rows, cols), jnp.bfloat16),
+        out_shape=jax.ShapeDtypeStruct((tiles, HD, BLK), jnp.bfloat16),
         in_specs=[vmem, vmem, vmem, smem, smem],
         out_specs=vmem,
         scratch_shapes=[
@@ -423,6 +436,15 @@
         ),
         name="line_attention",
     )(queries, prompt_kv, resp_kv, block_resp, block_pos)
+    some = heads // 2
+    return pl.pallas_call(
+        turn,
+        grid=(tiles // some,),
+        out_shape=jax.ShapeDtypeStruct((rows, cols), jnp.bfloat16),
+        in_specs=[pl.BlockSpec((some, HD, BLK), lambda i: (i, 0, 0))],
+        out_specs=pl.BlockSpec((BLK, some * HD), lambda i: (i // 2, i % 2)),
+        name="turn",
+    )(turned)
 
 
 def shards_of(queries, prompt_kv, resp_kv, block_resp, block_pos):

time: 76 us -> 74 us (0.974)
  local copies, waits for them, and re-layouts: 3.16 us -> 0 us
  Pallas kernels: 72.7 us -> 73.8 us
    unnamed x1 -> x0, local copies, waits for them, and re-layouts: 3.16 us -> none
    pallas_call x1 -> x2, Pallas kernels: 72.7 us -> 73.8 us  [the longest x1 69.7 us: line_of_four(): pl.pallas_call(kernel, out_shape=jax.ShapeDtypeStruct((tiles, HD, BLK), j...]
where the time goes in v2:
time: 74 us; the launch traced here: 73.8 us
  Pallas kernels  73.8 us (100%)
    pallas_call x1, Pallas kernels, line_of_four(): pl.pallas_call(kernel, out_shape=jax.ShapeDtypeStruct((tiles, HD, BLK), j...  69.7 us
    pallas_call x1, Pallas kernels, line_of_four(): pl.pallas_call(turn, grid=(tiles // some,), out_shape=jax.ShapeDtypeStruc...  4.14 us

profile of v2, /device:TPU:0, one launch (start us, length us, event | category | flops | bytes accessed | tf_op | source)
XLA Modules:
  0.0 73.8 jit_solution(13126953258802113943)
XLA Ops:
  0.0 69.7 %line_attention.1.x_ref = bf16[32,128,256]{2,1,0:T(8,128)(2,1)} custom-call(bf16[512,2048]{1,0:T(8,128)(2,1)} %q_ref.1, bf16[512,512]{1,0:T(8,128)(2,1)} %p_ref.1, bf16[512,512]{1,0:T(8,128)(2,1)} %r_ref.1, s32[8]{0:T(128)} %resp_ref.1, s32[8]{0:T(128)} %pos_ref.1), custom_call_target="tpu_custom_call" | custom-call | tf_op jit(solution)/shard_map/line_attention/pallas_call | solution.py:414
  69.7 4.1 %turn.1 = bf16[512,2048]{1,0:T(8,128)(2,1)} custom-call(bf16[32,128,256]{2,1,0:T(8,128)(2,1)} %line_attention.1.x_ref), custom_call_target="tpu_custom_call" | custom-call | tf_op jit(solution)/shard_map/turn/pallas_call | solution.py:440

commit v3 on v2

--- a/solution.py
+++ b/solution.py
@@ -307,22 +307,28 @@
         step = it // 4
         second = jnp.where(is_end, inner, other)
         third = jnp.where(is_end, jnp.where(low, 2, 1), near)
-        fourth = jnp.where(low, 3, 0)
-        src = jnp.where(
-            step == 0, me, jnp.where(step == 1, second, jnp.where(step == 2, third, fourth))
-        )
+        src = jnp.where(step == 0, me, jnp.where(step == 1, second, third))
         pl.when(it == 1)(lambda: event_early(1))
         at(it, 3, is_mid, lambda: event_entry(0))
         at(it, 6, is_mid, lambda: event_entry(1))
         at(it, 9, is_mid, lambda: event_far_p(0))
-        at(it, 13, is_mid, lambda: event_far_r(0))
-        at(it, 15, is_mid, lambda: event_far_r(1))
         at(it, 4, is_end, take_p(second))
         at(it, 8, is_end, take_p(third))
-        at(it, 12, is_end, take_p(fourth))
         slot, head = (it % 4) // 2, it % 2
         kc, vc = columns(head)
         attend(pb[src, :, kc], pb[src, :, vc], slot * 16 + head * 8)
+
+    def last_step(it):
+        half = it // 4
+        src = jnp.where(low, 3, 0)
+        at(it, 0, is_end, lambda: got_p(src, 0))
+        at(it, 4, is_end, lambda: got_p(src, 1))
+        at(it, 2, is_mid, lambda: event_far_r(0))
+        at(it, 5, is_mid, lambda: event_far_r(1))
+        slot, head = (it % 4) // 2, it % 2
+        kc, vc = columns(head)
+        rows = pl.ds(pl.multiple_of(half * BLK, BLK), BLK)
+        attend(pb[src, rows, kc], pb[src, rows, vc], slot * 16 + head * 8)
 
     def fill(k):
         used = []
@@ -373,7 +379,7 @@
 
     pl.when(is_mid)(lambda: event_far_p(1))
     fill(0)
-    pl.loop(12, 16)(prompt_step)
+    pl.loop(0, 8)(last_step)
     pl.when(is_end)(lambda: got_e(2))
     fill(1)
     pl.when(is_end)(lambda: got_e(3))

time: 74 us -> 73.5 us (level)
  no operation moved by 1% of the time
where the time goes in v3:
time: 73.5 us; the launch traced here: 73.3 us
  Pallas kernels  73.3 us (100%)
    pallas_call x1, Pallas kernels, line_of_four(): pl.pallas_call(kernel, out_shape=jax.ShapeDtypeStruct((tiles, HD, BLK), j...  69.2 us
    pallas_call x1, Pallas kernels, line_of_four(): pl.pallas_call(turn, grid=(tiles // some,), out_shape=jax.ShapeDtypeStruc...  4.14 us

profile of v3, /device:TPU:0, one launch (start us, length us, event | category | flops | bytes accessed | tf_op | source)
XLA Modules:
  0.0 73.3 jit_solution(7662305453163444417)
XLA Ops:
  0.0 69.2 %line_attention.1.x_ref = bf16[32,128,256]{2,1,0:T(8,128)(2,1)} custom-call(bf16[512,2048]{1,0:T(8,128)(2,1)} %q_ref.1, bf16[512,512]{1,0:T(8,128)(2,1)} %p_ref.1, bf16[512,512]{1,0:T(8,128)(2,1)} %r_ref.1, s32[8]{0:T(128)} %resp_ref.1, s32[8]{0:T(128)} %pos_ref.1), custom_call_target="tpu_custom_call" | custom-call | tf_op jit(solution)/shard_map/line_attention/pallas_call | solution.py:420
  69.2 4.1 %turn.1 = bf16[512,2048]{1,0:T(8,128)(2,1)} custom-call(bf16[32,128,256]{2,1,0:T(8,128)(2,1)} %line_attention.1.x_ref), custom_call_target="tpu_custom_call" | custom-call | tf_op jit(solution)/shard_map/turn/pallas_call | solution.py:446
